TPU v7x, 512 devices: a whole 4x8x8 slice. The times are simulated.
512 devices in a mesh: alpha: 32 (over x, z), beta: 16 (over y, core).
Axes of the slice: x: 4, y: 8, z: 8, core: 2. Of those that a mesh axis runs over, the one named last changes fastest.
Arguments:
- coef: bfloat16 [2, 4096, 32768], P(None, 'alpha', 'beta'), may hold values from -6 to 6
- alpha_diag: float32 [4096], P('alpha'), may hold values from -1 to 1
- beta_diag: float32 [32768], P('beta'), may hold values from -1 to 1
- alpha_tiles: bfloat16 [16, 128, 128], replicated, may hold values from -0.25 to 0.25
- beta_tiles: bfloat16 [16, 128, 128], replicated, may hold values from -0.125 to 0.125
- occupancy: int32 [32, 256], P('alpha', 'beta'), may hold values 0 or 1
- alpha_source: int32 [32, 4], replicated, may hold values from 0 to 31
- alpha_kind: int32 [32, 4], replicated, may hold values from 0 to 15
- alpha_parity: int32 [32, 4], replicated, may hold values from 0 to 1
- slot_device: int32 [256, 1], replicated, may hold values from 0 to 15; in each aligned block of 16 rows (0 to 15, 16 to 31, ...) at most 2 rows name the same one
- slot_offset: int32 [256], replicated, may hold values from 0 to 15
- beta_slot: int32 [256, 16], P('beta'), may hold values from 0 to 15
- beta_kind: int32 [256, 16], P('beta'), may hold values from 0 to 15
- beta_parity: int32 [256, 16], P('beta'), may hold values from 0 to 1
- mixed_block: int32 [16], P('beta'), may hold values from 0 to 15
- mixed_kind: int32 [16], P('beta'), may hold values from 0 to 15
Outputs:
- sigma: bfloat16 [2, 4096, 32768], P(None, 'alpha', 'beta')
Inputs may be any that keep to these rules, and one draw needn't show every extreme that they name: `slot_device`: in each aligned block of 16 rows (the slots of one beta index) no number appears in more than 2 rows, and in some block one appears in exactly 2 rows.
All inputs are finite; a program needn't handle non-finite values. No bound on the sum of `occupancy` on one device may be relied on, other than what follows from the above.
Results may differ from a plain program's by a relative error of at most 0.0018.
Values may be sent and summed in bfloat16 or wider, within the bound.
A program may use at most 64 MiB of HBM per device.

v0:
```python
import functools

import jax
import jax.numpy as jnp
from jax import lax
from jax.experimental import pallas as pl
from jax.experimental.pallas import tpu as pltpu
from jax.sharding import PartitionSpec as P

MESH = pl.DeviceIdType.MESH
BLK = 128
NBLK = 16
SLOTS = 16
EB = 16
EA = 4
ROWS = 2 * BLK
ORDERS = {
    4: ((1, 2), (1, 1), (2, 2)),
    8: ((1, 4), (1, 3), (1, 2), (2, 4), (2, 3), (1, 1), (3, 4), (2, 2), (3, 3), (4, 4)),
}
IN_FLIGHT = 3
F32 = jnp.float32
BF16 = jnp.bfloat16


def kernel(X, Z, Y, *refs):
    small_hbm, (coef_hbm, at_hbm, bt_hbm, out), small = refs[:13], refs[13:17], refs[17:30]
    occ, asrc, akind, apar, sdev, soff, bslot, bkind, bpar, mblk, mkind, ad, bd = small
    coef, at, bt, panels, share, shares, adiag, mixed, locs, send, recv, passing, wide, products, stash = refs[30:45]
    (
        small_sem,
        local_sem,
        send_sem,
        recv_sem,
        side_sem,
        zsend_sem,
        zrecv_sem,
        xsend_sem,
        xrecv_sem,
    ) = refs[45:]
    NB = 2 * Y
    me_a = lax.axis_index("alpha")
    me_b = lax.axis_index("beta")
    x, z = me_a // Z, lax.rem(me_a, Z)
    y, c = me_b // 2, lax.rem(me_b, 2)

    small_loads = [
        pltpu.make_async_copy(src, dst, small_sem.at[i]) for i, (src, dst) in enumerate(zip(small_hbm, small))
    ]
    for load in small_loads:
        load.start()

    def block_load(j):
        columns = pl.ds(pl.multiple_of(j * BLK, BLK), BLK)
        return pltpu.make_async_copy(coef_hbm.at[:, columns], coef.at[j], local_sem.at[j])

    tile_loads = [
        pltpu.make_async_copy(at_hbm, at.at[pl.ds(0, 16)], local_sem.at[NBLK]),
        pltpu.make_async_copy(bt_hbm, bt, local_sem.at[NBLK + 1]),
    ]

    def load_block(j, _):
        block_load(j).start()
        return 0

    lax.fori_loop(0, NBLK, load_block, 0)
    for load in tile_loads:
        load.start()

    def peer(p, flip):
        dist = (Y - p) // 2
        dy = jnp.where(lax.rem(p, 2) == 1, dist, Y - dist)
        return lax.rem(y + dy, Y) * 2 + lax.rem(c + flip, 2)

    M = Y // 2
    own = Y - 1
    order = ORDERS[Y]
    up, down = lax.rem(y + 1, Y) * 2, lax.rem(y + Y - 1, Y) * 2

    barrier = pltpu.get_barrier_semaphore()

    for neighbour in (up, up + 1, down, down + 1, y * 2 + 1 - c):
        pl.semaphore_signal(barrier, 1, device_id=(me_a, neighbour), device_id_type=MESH)

    has_next, has_prev = z < Z - 1, z > 0

    @pl.when(has_next)
    def _():
        pl.semaphore_signal(barrier, 1, device_id=(me_a + 1, me_b), device_id_type=MESH)

    @pl.when(has_prev)
    def _():
        pl.semaphore_signal(barrier, 1, device_id=(me_a - 1, me_b), device_id_type=MESH)

    def greet_x(i, _):
        pl.semaphore_signal(barrier, 1, device_id=(lax.rem(x + i, X) * Z + z, me_b), device_id_type=MESH)
        return 0

    lax.fori_loop(1, X, greet_x, 0)

    for load in small_loads:
        load.wait()

    def await_block(j, _):
        block_load(j).wait()
        return 0

    lax.fori_loop(0, NBLK, await_block, 0)

    def panel_of(block, allowed):
        panel = coef[block]
        return jnp.where(allowed, panel, jnp.zeros_like(panel))

    active = mblk[0]
    mine = panel_of(active, occ[0, active] > 0)
    panels[z] = jnp.concatenate([mine[:BLK], mine[BLK:]], axis=1)

    def pack(p):
        def one(flip, _):
            d = peer(p, flip)
            code = jnp.int32(0)
            for i in range(SLOTS):
                hit = sdev[d * SLOTS + i] == me_b
                code = jnp.where(hit, code * 32 + soff[d * SLOTS + i] + 1, code)
            hi, lo = code >> 5, code & 31
            first = jnp.where(hi > 0, hi, lo)
            second = jnp.where(hi > 0, lo, 0)
            for r, named in enumerate((first, second)):
                block = jnp.clip(named - 1, 0, NBLK - 1)
                panel = panel_of(block, (named > 0) & (occ[0, block] > 0))
                place = (flip + 2 * r) if p == 0 else (4 * p + 2 * flip + r)
                for h in range(2):
                    send[h, place] = panel[h * BLK : (h + 1) * BLK]
            return 0

        lax.fori_loop(0, 2, one, 0)

    pl.semaphore_wait(barrier, 5 + X - 1 + jnp.where(has_next, 1, 0) + jnp.where(has_prev, 1, 0))

    places, count = {}, 0
    for hop in range(1, M):
        for dist in range(M, hop, -1):
            places[hop, dist] = count
            count += 2 if dist == M else 4

    L = len(order)

    def message(way, g):
        h, i = divmod(g, L)
        hop, dist = order[i]
        p = 0 if dist == M else Y - 1 - 2 * dist if way == 0 else Y - 2 * dist
        size = 2 if dist == M else 4
        first = 2 * way if dist == M else 4 * p
        chip = up if way == 0 else down

        def leg(src, at_, dst, to_at, length, core, flip):
            return pltpu.make_async_remote_copy(
                src_ref=src.at[pl.ds(at_, length)],
                dst_ref=dst.at[pl.ds(to_at, length)],
                send_sem=send_sem.at[way, g, flip],
                recv_sem=recv_sem.at[way, g, flip],
                device_id=(me_a, chip + core),
                device_id_type=MESH,
            )

        src, begin = (send.at[h], first) if hop == 1 else (passing.at[h, way], places[hop - 1, dist])
        if hop < dist:
            return [leg(src, begin, passing.at[h, way], places[hop, dist], size, c, 0)]
        half = size // 2
        return [
            leg(src, begin + half * flip, recv.at[h], first + half * flip, half, lax.rem(c + flip, 2), flip)
            for flip in range(2)
        ]

    def side_copy():
        return pltpu.make_async_remote_copy(
            src_ref=send.at[:, pl.ds(4 * own + 2, 2)],
            dst_ref=recv.at[:, pl.ds(4 * own + 2, 2)],
            send_sem=side_sem.at[0],
            recv_sem=side_sem.at[1],
            device_id=(me_a, y * 2 + 1 - c),
            device_id_type=MESH,
        )

    def advance(g):
        h, i = divmod(g, L)
        hop, dist = order[i]
        for way in range(2):
            if hop > 1:
                for copy in message(way, h * L + order.index((hop - 1, dist))):
                    copy.wait_recv()
            if g >= IN_FLIGHT:
                for copy in message(way, g - IN_FLIGHT):
                    copy.wait_send()
            for copy in message(way, g):
                copy.start()

    def expand(h, first, count):
        def two(n, _):
            start = first + 2 * n
            rows = recv[h, pl.ds(start, 2)].reshape(ROWS, BLK)

            def pair(q, _):
                result = jnp.dot(rows, wide[q], preferred_element_type=F32)
                for a in range(2):
                    for b in range(2):
                        products[start + a, 2 * q + b] = result[a * BLK : (a + 1) * BLK, b * BLK : (b + 1) * BLK]
                return 0

            lax.fori_loop(0, 8, pair, 0, unroll=4)
            return 0

        lax.fori_loop(0, count // 2, two, 0)

    def land(g):
        h, i = divmod(g, L)
        hop, dist = order[i]
        for way in range(2):
            for copy in message(way, g):
                copy.wait_recv()
        if dist == M:
            expand(h, 0, 4)
        else:
            expand(h, 4 * (Y - 1 - 2 * dist), 8)

    def panel_copy(way, s):
        origin, to = (z - s + 1, me_a + 1) if way == 0 else (z + s - 1, me_a - 1)
        origin = jnp.clip(origin, 0, Z - 1)
        return pltpu.make_async_remote_copy(
            src_ref=panels.at[origin],
            dst_ref=panels.at[origin],
            send_sem=zsend_sem.at[way, s],
            recv_sem=zrecv_sem.at[way, s],
            device_id=(to, me_b),
            device_id_type=MESH,
        )

    def panel_leaves(way, s):
        return (z - s + 1 >= 0) & has_next if way == 0 else (z + s - 1 < Z) & has_prev

    def panel_arrives(way, s):
        return z - s >= 0 if way == 0 else z + s < Z

    def start_panels(s):
        for way in range(2):

            @pl.when(panel_leaves(way, s))
            def _():
                panel_copy(way, s).start()

    def await_panels(s):
        for way in range(2):

            @pl.when(panel_arrives(way, s))
            def _():
                origin = jnp.clip(z - s if way == 0 else z + s, 0, Z - 1)
                pltpu.make_async_remote_copy(
                    src_ref=panels.at[origin],
                    dst_ref=panels.at[origin],
                    send_sem=zsend_sem.at[way, s],
                    recv_sem=zrecv_sem.at[way, s],
                    device_id=(jnp.where(has_next, me_a + 1, me_a - 1), me_b),
                    device_id_type=MESH,
                ).wait_recv()

    def sent_panels(s):
        for way in range(2):

            @pl.when(panel_leaves(way, s))
            def _():
                panel_copy(way, s).wait_send()

    def share_copy(i):
        return pltpu.make_async_remote_copy(
            src_ref=share.at[i],
            dst_ref=shares.at[i],
            send_sem=xsend_sem.at[i],
            recv_sem=xrecv_sem.at[i],
            device_id=(lax.rem(x + i, X) * Z + z, me_b),
            device_id_type=MESH,
        )

    def next_panels(s):
        if s < Z:
            await_panels(s)
        if s + 1 < Z:
            start_panels(s + 1)

    started = 0
    for p in range(Y):
        pack(p)
        if p == 0 and Z > 1:
            start_panels(1)
        if p % 2 == 0 and started < IN_FLIGHT and order[started][0] == 1:
            advance(started)
            started += 1
    side_copy().start()
    recv[:, pl.ds(4 * own, 2)] = send[:, pl.ds(4 * own, 2)]

    def placed(i, _):
        s = sdev[me_b * SLOTS + i]
        rank = jnp.int32(0)
        for other in range(SLOTS):
            same = (sdev[me_b * SLOTS + other] == s) & (other < i)
            rank = rank + jnp.where(same, 1, 0)
        dy = lax.rem(y - (s >> 1) + Y, Y)
        p = jnp.where(dy < Y // 2, Y - 1 - 2 * dy, 2 * dy - Y)
        flip = (s + c) & 1
        rank = jnp.minimum(rank, 1)
        locs[i] = jnp.where(p == 0, flip + 2 * rank, 4 * p + 2 * flip + rank)
        return 0

    lax.fori_loop(0, SLOTS, placed, 0)

    adiag[...] = jnp.broadcast_to(ad[...], (BLK, BLK)).T

    for load in tile_loads:
        load.wait()

    def negate(i, _):
        at[16 + i] = -at[i]
        return 0

    lax.fori_loop(0, 16, negate, 0)
    at[32] = jnp.zeros((BLK, BLK), BF16)

    def widen(q, _):
        wide[q] = jnp.concatenate([bt[2 * q], bt[2 * q + 1]], axis=1)
        return 0

    lax.fori_loop(0, 8, widen, 0)

    def share_of(i):
        target = lax.rem(x + i, X) * Z + z
        tiles, sources = [], []
        for e in range(EA):
            s = asrc[e, target]
            here = lax.div(s, Z) == x
            tiles.append(at[jnp.where(here, akind[e, target] + 16 * apar[e, target], 32)])
            sources.append(panels[lax.rem(s, Z)])
        return jnp.dot(
            jnp.concatenate(tiles, axis=1), jnp.concatenate(sources, axis=0), preferred_element_type=F32
        )

    def give_shares():
        for i in range(1, X):
            share[i] = share_of(i).astype(BF16)
            share_copy(i).start()

    def close_mixed():
        inner = share_of(0)
        for i in range(1, X):
            share_copy(i).wait_recv()
            inner = inner + shares[i].astype(F32)
        inner = jnp.concatenate([inner[:, :BLK], inner[:, BLK:]], axis=0)
        coarse = inner.astype(BF16)
        fine = (inner - coarse.astype(F32)).astype(BF16)
        closing = bt[mkind[0]]
        mixed[...] = jnp.dot(
            jnp.concatenate([coarse, fine], axis=1),
            jnp.concatenate([closing, closing], axis=0),
            preferred_element_type=F32,
        )

    def finish(h):
        rows = pl.ds(h * BLK, BLK)

        def block(j, _):
            columns = pl.ds(pl.multiple_of(j * BLK, BLK), BLK)
            struck = jnp.where(j == active, 1.0, 0.0).astype(F32)
            total = (adiag[...] + bd[pl.ds(j, 1), :]) * coef[j, rows, :].astype(F32)
            if h == 1:
                total = total + struck * mixed[rows, :]
            for e in range(EB):
                sign = (1 - 2 * bpar[j, e]).astype(F32)
                total = total + sign * products[locs[bslot[j, e]], bkind[j, e]]
            if h == 0:
                stash[...] = stash[...] + struck * total
            out[rows, columns] = (total * occ[0, j].astype(F32)).astype(BF16)
            return 0

        lax.fori_loop(0, NBLK, block, 0)

    def amend():
        rows = pl.ds(0, BLK)
        whole = ((stash[...] + mixed[rows, :]) * occ[0, active].astype(F32)).astype(BF16)

        def block(j, _):
            columns = pl.ds(pl.multiple_of(j * BLK, BLK), BLK)
            out[rows, columns] = jnp.where(j == active, whole, out[rows, columns])
            return 0

        lax.fori_loop(0, NBLK, block, 0)

    def first_plane():
        stash[...] = jnp.zeros((BLK, BLK), F32)
        finish(0)
        expand(1, 4 * own, 4)

    beside = []
    for n, (hop, dist) in enumerate(order):
        if hop == dist:
            beside.append((n + IN_FLIGHT, functools.partial(land, n)))
            beside.append((L + n + IN_FLIGHT, functools.partial(land, L + n)))
    beside.append((started, functools.partial(expand, 0, 4 * own, 2)))

    def beside_core():
        side_copy().wait_recv()
        expand(0, 4 * own + 2, 2)

    beside.append((started + 1, beside_core))
    beside.append((L + IN_FLIGHT - 1, first_plane))
    for s in range(1, Z):
        beside.append((started + 2 * (s - 1), functools.partial(next_panels, s)))
    late = 2 * L - 2
    beside.append((late - 2, give_shares))
    beside.append((late, close_mixed))
    beside.append((late + 1, amend))
    beside.sort(key=lambda entry: entry[0])
    for g in range(started, 2 * L):
        advance(g)
        while beside and beside[0][0] <= g:
            beside.pop(0)[1]()
    for _, work in beside:
        work()
    finish(1)

    side_copy().wait_send()
    for g in range(2 * L - IN_FLIGHT, 2 * L):
        for way in range(2):
            for copy in message(way, g):
                copy.wait_send()

    def left_panels(s, _):
        sent_panels(s)
        return 0

    lax.fori_loop(1, Z, left_panels, 0)
    for i in range(1, X):
        share_copy(i).wait_send()


def solution(mesh):
    n_alpha, n_beta = mesh.shape["alpha"], mesh.shape["beta"]
    Z = 8 if n_alpha == 32 else 1
    X, Y = n_alpha // Z, n_beta // 2
    waiting = sum(2 if 2 * dist == Y else 4 for hop, dist in ORDERS[Y] if hop < dist)

    def local(
        coef,
        alpha_diag,
        beta_diag,
        alpha_tiles,
        beta_tiles,
        occupancy,
        alpha_source,
        alpha_kind,
        alpha_parity,
        slot_device,
        slot_offset,
        beta_slot,
        beta_kind,
        beta_parity,
        mixed_block,
        mixed_kind,
    ):
        vmem = pl.BlockSpec(memory_space=pltpu.VMEM)
        hbm = pl.BlockSpec(memory_space=pl.ANY)
        columns = coef.shape[-1]
        small = (
            occupancy,
            alpha_source.T,
            alpha_kind.T,
            alpha_parity.T,
            slot_device.reshape(-1),
            slot_offset,
            beta_slot,
            beta_kind,
            beta_parity,
            mixed_block,
            mixed_kind,
            alpha_diag.reshape(1, BLK),
            beta_diag.reshape(NBLK, BLK),
        )
        result = pl.pallas_call(
            functools.partial(kernel, X, Z, Y),
            out_shape=jax.ShapeDtypeStruct((ROWS, columns), BF16),
            in_specs=[hbm] * (len(small) + 3),
            out_specs=vmem,
            scratch_shapes=[
                *(pltpu.SMEM(v.shape, v.dtype) for v in small[:11]),
                *(pltpu.VMEM(v.shape, v.dtype) for v in small[11:]),
                pltpu.VMEM((NBLK, ROWS, BLK), BF16),
                pltpu.VMEM((33, BLK, BLK), BF16),
                pltpu.VMEM((16, BLK, BLK), BF16),
                pltpu.VMEM((Z, BLK, ROWS), BF16),
                pltpu.VMEM((X, BLK, ROWS), BF16),
                pltpu.VMEM((X, BLK, ROWS), BF16),
                pltpu.VMEM((BLK, BLK), F32),
                pltpu.VMEM((ROWS, BLK), F32),
                pltpu.SMEM((SLOTS,), jnp.int32),
                pltpu.VMEM((2, 2 * n_beta, BLK, BLK), BF16),
                pltpu.VMEM((2, 2 * n_beta, BLK, BLK), BF16),
                pltpu.VMEM((2, 2, waiting, BLK, BLK), BF16),
                pltpu.VMEM((8, BLK, 2 * BLK), BF16),
                pltpu.VMEM((2 * n_beta, 16, BLK, BLK), F32),
                pltpu.VMEM((BLK, BLK), F32),
                pltpu.SemaphoreType.DMA((len(small),)),
                pltpu.SemaphoreType.DMA((NBLK + 2,)),
                pltpu.SemaphoreType.DMA((2, 2 * len(ORDERS[Y]), 2)),
                pltpu.SemaphoreType.DMA((2, 2 * len(ORDERS[Y]), 2)),
                pltpu.SemaphoreType.DMA((2,)),
                pltpu.SemaphoreType.DMA((2, Z)),
                pltpu.SemaphoreType.DMA((2, Z)),
                pltpu.SemaphoreType.DMA((X,)),
                pltpu.SemaphoreType.DMA((X,)),
            ],
            compiler_params=pltpu.CompilerParams(
                collective_id=0, has_side_effects=True, vmem_limit_bytes=60 * 1024 * 1024
            ),
            cost_estimate=pl.CostEstimate(flops=2200000000, bytes_accessed=3300000, transcendentals=0),
        )(
            *small,
            coef.reshape(ROWS, columns),
            alpha_tiles,
            beta_tiles,
        )
        return result.reshape(coef.shape)

    in_specs = (
        P(None, "alpha", "beta"),
        P("alpha"),
        P("beta"),
        P(),
        P(),
        P("alpha", "beta"),
        P(),
        P(),
        P(),
        P(),
        P(),
        P("beta", None),
        P("beta", None),
        P("beta", None),
        P("beta"),
        P("beta"),
    )
    out_specs = P(None, "alpha", "beta")
    return jax.shard_map(local, mesh=mesh, in_specs=in_specs, out_specs=out_specs, check_vma=False)
```

profile of v0, /device:TPU:1, one launch (start us, length us, event | category | flops | bytes accessed | tf_op | source)
XLA Modules:
  0.0 67.1 jit_solution(15057195085421785538)
XLA Ops:
  1.3 63.5 %shard_map.154 = bf16[256,2048]{1,0:T(8,128)(2,1)} custom-call(s32[1,16]{1,0:T(1,128)} %refs_0_.1, s32[4,32]{1,0:T(4,128)} %bitcast.11, s32[4,32]{1,0:T(4,128)} %bitcast.12, s32[4,32]{1,0:T(4,128)} %bitcast.13, s32[256]{0:T(256)} %bitcast.14, s32[256]{0:T(256)} %refs_5_.1, s32[16,16]{1,0:T(8,128)} %refs_6_.1, s32[16,16]{1,0:T(8,128)} %refs_7_.1, ...), custom_call_target="tpu_custom_call" | custom-call | flops 2200000000 | bytes 3300000 | tf_op jit(solution)/shard_map/pallas_call | solution.py:485
  64.8 2.3 %copy.20 = bf16[2,128,2048]{2,1,0:T(8,128)(2,1)} copy(bf16[2,128,2048]{2,1,0:T(8,128)(2,1)} %bitcast.8) | data formatting | bytes 2097152
where the time goes:
time: 67.3 us; the launch traced here: 67.1 us
  Pallas kernels  63.5 us (94%)
  local copies, waits for them, and re-layouts  2.3 us (3%)
  between operations  1.3 us (2%)
    pallas_call x1, Pallas kernels, local(): pl.pallas_call(functools.partial(kernel, X, Z, Y), out_shape=jax.ShapeDty...  63.5 us
    unnamed x1, local copies, waits for them, and re-layouts  2.3 us

commit v1 on v0

--- a/solution.py
+++ b/solution.py
@@ -24,11 +24,12 @@
 
 
 def kernel(X, Z, Y, *refs):
-    small_hbm, (coef_hbm, at_hbm, bt_hbm, out), small = refs[:13], refs[13:17], refs[17:30]
-    occ, asrc, akind, apar, sdev, soff, bslot, bkind, bpar, mblk, mkind, ad, bd = small
-    coef, at, bt, panels, share, shares, adiag, mixed, locs, send, recv, passing, wide, products, stash = refs[30:45]
+    small_hbm, (coef_hbm, at_hbm, bt_hbm, out_hbm), small = refs[:13], refs[13:17], refs[17:30]
+    occ, sdev, soff, mblk, mkind, asrc, akind, apar, bslot, bkind, bpar, ad, bd = small
+    coef, at, bt, panels, share, shares, adiag, mixed, locs, send, recv, passing, wide, products, stash, out = refs[30:46]
     (
         small_sem,
+        out_sem,
         local_sem,
         send_sem,
         recv_sem,
@@ -37,17 +38,48 @@
         zrecv_sem,
         xsend_sem,
         xrecv_sem,
-    ) = refs[45:]
+    ) = refs[46:]
     NB = 2 * Y
     me_a = lax.axis_index("alpha")
     me_b = lax.axis_index("beta")
     x, z = me_a // Z, lax.rem(me_a, Z)
     y, c = me_b // 2, lax.rem(me_b, 2)
 
+    def peer(p, flip):
+        dist = (Y - p) // 2
+        dy = jnp.where(lax.rem(p, 2) == 1, dist, Y - dist)
+        return lax.rem(y + dy, Y) * 2 + lax.rem(c + flip, 2)
+
+    M = Y // 2
+    own = Y - 1
+    order = ORDERS[Y]
+    up, down = lax.rem(y + 1, Y) * 2, lax.rem(y + Y - 1, Y) * 2
+
+    barrier = pltpu.get_barrier_semaphore()
+
+    for neighbour in (up, up + 1, down, down + 1, y * 2 + 1 - c):
+        pl.semaphore_signal(barrier, 1, device_id=(me_a, neighbour), device_id_type=MESH)
+
+    has_next, has_prev = z < Z - 1, z > 0
+
+    @pl.when(has_next)
+    def _():
+        pl.semaphore_signal(barrier, 1, device_id=(me_a + 1, me_b), device_id_type=MESH)
+
+    @pl.when(has_prev)
+    def _():
+        pl.semaphore_signal(barrier, 1, device_id=(me_a - 1, me_b), device_id_type=MESH)
+
+    def greet_x(i, _):
+        pl.semaphore_signal(barrier, 1, device_id=(lax.rem(x + i, X) * Z + z, me_b), device_id_type=MESH)
+        return 0
+
+    lax.fori_loop(1, X, greet_x, 0)
+
     small_loads = [
         pltpu.make_async_copy(src, dst, small_sem.at[i]) for i, (src, dst) in enumerate(zip(small_hbm, small))
     ]
-    for load in small_loads:
+    for load in small_loads[:4]:
         load.start()
 
     def block_load(j):
@@ -64,41 +96,9 @@
         return 0
 
     lax.fori_loop(0, NBLK, load_block, 0)
-    for load in tile_loads:
+    for load in small_loads[4:] + tile_loads:
         load.start()
-
-    def peer(p, flip):
-        dist = (Y - p) // 2
-        dy = jnp.where(lax.rem(p, 2) == 1, dist, Y - dist)
-        return lax.rem(y + dy, Y) * 2 + lax.rem(c + flip, 2)
-
-    M = Y // 2
-    own = Y - 1
-    order = ORDERS[Y]
-    up, down = lax.rem(y + 1, Y) * 2, lax.rem(y + Y - 1, Y) * 2
-
-    barrier = pltpu.get_barrier_semaphore()
-
-    for neighbour in (up, up + 1, down, down + 1, y * 2 + 1 - c):
-        pl.semaphore_signal(barrier, 1, device_id=(me_a, neighbour), device_id_type=MESH)
-
-    has_next, has_prev = z < Z - 1, z > 0
-
-    @pl.when(has_next)
-    def _():
-        pl.semaphore_signal(barrier, 1, device_id=(me_a + 1, me_b), device_id_type=MESH)
-
-    @pl.when(has_prev)
-    def _():
-        pl.semaphore_signal(barrier, 1, device_id=(me_a - 1, me_b), device_id_type=MESH)
-
-    def greet_x(i, _):
-        pl.semaphore_signal(barrier, 1, device_id=(lax.rem(x + i, X) * Z + z, me_b), device_id_type=MESH)
-        return 0
-
-    lax.fori_loop(1, X, greet_x, 0)
-
-    for load in small_loads:
+    for load in small_loads[:4]:
         load.wait()
 
     def await_block(j, _):
@@ -135,6 +135,7 @@
 
         lax.fori_loop(0, 2, one, 0)
 
+    pack(0)
     pl.semaphore_wait(barrier, 5 + X - 1 + jnp.where(has_next, 1, 0) + jnp.where(has_prev, 1, 0))
 
     places, count = {}, 0
@@ -288,7 +289,8 @@
 
     started = 0
     for p in range(Y):
-        pack(p)
+        if p > 0:
+            pack(p)
         if p == 0 and Z > 1:
             start_panels(1)
         if p % 2 == 0 and started < IN_FLIGHT and order[started][0] == 1:
@@ -296,6 +298,9 @@
             started += 1
     side_copy().start()
     recv[:, pl.ds(4 * own, 2)] = send[:, pl.ds(4 * own, 2)]
+
+    for load in small_loads[4:]:
+        load.wait()
 
     def placed(i, _):
         s = sdev[me_b * SLOTS + i]
@@ -362,6 +367,12 @@
             preferred_element_type=F32,
         )
 
+    QUARTER = NBLK // 4
+
+    def written(h, part):
+        view = (pl.ds(h * BLK, BLK), pl.ds(part * QUARTER * BLK, QUARTER * BLK))
+        return pltpu.make_async_copy(out.at[view], out_hbm.at[view], out_sem.at[h, part])
+
     def finish(h):
         rows = pl.ds(h * BLK, BLK)
 
@@ -379,7 +390,10 @@
             out[rows, columns] = (total * occ[0, j].astype(F32)).astype(BF16)
             return 0
 
-        lax.fori_loop(0, NBLK, block, 0)
+        for part in range(4):
+            lax.fori_loop(part * QUARTER, (part + 1) * QUARTER, block, 0)
+            if h == 1:
+                written(1, part).start()
 
     def amend():
         rows = pl.ds(0, BLK)
@@ -391,6 +405,8 @@
             return 0
 
         lax.fori_loop(0, NBLK, block, 0)
+        for part in range(4):
+            written(0, part).start()
 
     def first_plane():
         stash[...] = jnp.zeros((BLK, BLK), F32)
@@ -426,6 +442,9 @@
     finish(1)
 
     side_copy().wait_send()
+    for h in range(2):
+        for part in range(4):
+            written(h, part).wait()
     for g in range(2 * L - IN_FLIGHT, 2 * L):
         for way in range(2):
             for copy in message(way, g):
@@ -464,21 +483,20 @@
         mixed_block,
         mixed_kind,
     ):
-        vmem = pl.BlockSpec(memory_space=pltpu.VMEM)
         hbm = pl.BlockSpec(memory_space=pl.ANY)
         columns = coef.shape[-1]
         small = (
             occupancy,
+            slot_device.reshape(-1),
+            slot_offset,
+            mixed_block,
+            mixed_kind,
             alpha_source.T,
             alpha_kind.T,
             alpha_parity.T,
-            slot_device.reshape(-1),
-            slot_offset,
             beta_slot,
             beta_kind,
             beta_parity,
-            mixed_block,
-            mixed_kind,
             alpha_diag.reshape(1, BLK),
             beta_diag.reshape(NBLK, BLK),
         )
@@ -486,7 +504,7 @@
             functools.partial(kernel, X, Z, Y),
             out_shape=jax.ShapeDtypeStruct((ROWS, columns), BF16),
             in_specs=[hbm] * (len(small) + 3),
-            out_specs=vmem,
+            out_specs=hbm,
             scratch_shapes=[
                 *(pltpu.SMEM(v.shape, v.dtype) for v in small[:11]),
                 *(pltpu.VMEM(v.shape, v.dtype) for v in small[11:]),
@@ -505,7 +523,9 @@
                 pltpu.VMEM((8, BLK, 2 * BLK), BF16),
                 pltpu.VMEM((2 * n_beta, 16, BLK, BLK), F32),
                 pltpu.VMEM((BLK, BLK), F32),
+                pltpu.VMEM((ROWS, columns), BF16),
                 pltpu.SemaphoreType.DMA((len(small),)),
+                pltpu.SemaphoreType.DMA((2, 4)),
                 pltpu.SemaphoreType.DMA((NBLK + 2,)),
                 pltpu.SemaphoreType.DMA((2, 2 * len(ORDERS[Y]), 2)),
                 pltpu.SemaphoreType.DMA((2, 2 * len(ORDERS[Y]), 2)),

time: 67.3 us -> 66.8 us (level)
  no operation moved by 1% of the time
where the time goes in v1:
time: 66.8 us; the launch traced here: 66.6 us
  Pallas kernels  63 us (94%)
  local copies, waits for them, and re-layouts  2.3 us (3%)
  between operations  1.3 us (2%)
    pallas_call x1, Pallas kernels, local(): pl.pallas_call(functools.partial(kernel, X, Z, Y), out_shape=jax.ShapeDty...  63 us
    unnamed x1, local copies, waits for them, and re-layouts  2.3 us

profile of v1, /device:TPU:1, one launch (start us, length us, event | category | flops | bytes accessed | tf_op | source)
XLA Modules:
  0.0 66.6 jit_solution(9342695002307233330)
XLA Ops:
  1.3 63.0 %shard_map.154 = bf16[256,2048]{1,0:T(8,128)(2,1)} custom-call(s32[1,16]{1,0:T(1,128)} %refs_0_.1, s32[256]{0:T(256)} %bitcast.14, s32[256]{0:T(256)} %refs_2_.1, s32[1]{0:T(128)S(6)} %copy.18.refs_3_, s32[1]{0:T(128)S(6)} %copy.19.refs_4_, s32[4,32]{1,0:T(4,128)} %bitcast.11, s32[4,32]{1,0:T(4,128)} %bitcast.12, s32[4,32]{1,0:T(4,128)} %bitcast.13, ...), custom_call_target="tpu_custom_call" | custom-call | flops 2200000000 | bytes 3300000 | tf_op jit(solution)/shard_map/pallas_call | solution.py:503
  64.3 2.3 %copy.20 = bf16[2,128,2048]{2,1,0:T(8,128)(2,1)} copy(bf16[2,128,2048]{2,1,0:T(8,128)(2,1)} %bitcast.8) | data formatting | bytes 2097152

commit v2 on v1

--- a/solution.py
+++ b/solution.py
@@ -16,7 +16,7 @@
 ROWS = 2 * BLK
 ORDERS = {
     4: ((1, 2), (1, 1), (2, 2)),
-    8: ((1, 4), (1, 3), (1, 2), (2, 4), (2, 3), (1, 1), (3, 4), (2, 2), (3, 3), (4, 4)),
+    8: ((1, 4), (1, 3), (1, 2), (2, 4), (2, 3), (2, 2), (1, 1), (3, 4), (3, 3), (4, 4)),
 }
 IN_FLIGHT = 3
 F32 = jnp.float32
@@ -26,7 +26,7 @@
 def kernel(X, Z, Y, *refs):
     small_hbm, (coef_hbm, at_hbm, bt_hbm, out_hbm), small = refs[:13], refs[13:17], refs[17:30]
     occ, sdev, soff, mblk, mkind, asrc, akind, apar, bslot, bkind, bpar, ad, bd = small
-    coef, at, bt, panels, share, shares, adiag, mixed, locs, send, recv, passing, wide, products, stash, out = refs[30:46]
+    coef, at, bt, panels, share, shares, adiag, mixed, locs, send, recv, passing, wide, products, stash, out, plan, signs = refs[30:48]
     (
         small_sem,
         out_sem,
@@ -38,7 +38,7 @@
         zrecv_sem,
         xsend_sem,
         xrecv_sem,
-    ) = refs[46:]
+    ) = refs[48:]
     NB = 2 * Y
     me_a = lax.axis_index("alpha")
     me_b = lax.axis_index("beta")
@@ -205,7 +205,7 @@
                 result = jnp.dot(rows, wide[q], preferred_element_type=F32)
                 for a in range(2):
                     for b in range(2):
-                        products[start + a, 2 * q + b] = result[a * BLK : (a + 1) * BLK, b * BLK : (b + 1) * BLK]
+                        products[(start + a) * 16 + 2 * q + b] = result[a * BLK : (a + 1) * BLK, b * BLK : (b + 1) * BLK]
                 return 0
 
             lax.fori_loop(0, 8, pair, 0, unroll=4)
@@ -383,8 +383,7 @@
             if h == 1:
                 total = total + struck * mixed[rows, :]
             for e in range(EB):
-                sign = (1 - 2 * bpar[j, e]).astype(F32)
-                total = total + sign * products[locs[bslot[j, e]], bkind[j, e]]
+                total = total + signs[j * EB + e] * products[plan[j * EB + e]]
             if h == 0:
                 stash[...] = stash[...] + struck * total
             out[rows, columns] = (total * occ[0, j].astype(F32)).astype(BF16)
@@ -407,6 +406,15 @@
         lax.fori_loop(0, NBLK, block, 0)
         for part in range(4):
             written(0, part).start()
+
+    def look_up():
+        def one(j, _):
+            for e in range(EB):
+                plan[j * EB + e] = locs[bslot[j, e]] * 16 + bkind[j, e]
+                signs[j * EB + e] = (1 - 2 * bpar[j, e]).astype(F32)
+            return 0
+
+        lax.fori_loop(0, NBLK, one, 0)
 
     def first_plane():
         stash[...] = jnp.zeros((BLK, BLK), F32)
@@ -425,6 +433,7 @@
         expand(0, 4 * own + 2, 2)
 
     beside.append((started + 1, beside_core))
+    beside.append((started + 1, look_up))
     beside.append((L + IN_FLIGHT - 1, first_plane))
     for s in range(1, Z):
         beside.append((started + 2 * (s - 1), functools.partial(next_panels, s)))
@@ -521,9 +530,11 @@
                 pltpu.VMEM((2, 2 * n_beta, BLK, BLK), BF16),
                 pltpu.VMEM((2, 2, waiting, BLK, BLK), BF16),
                 pltpu.VMEM((8, BLK, 2 * BLK), BF16),
-                pltpu.VMEM((2 * n_beta, 16, BLK, BLK), F32),
+                pltpu.VMEM((2 * n_beta * 16, BLK, BLK), F32),
                 pltpu.VMEM((BLK, BLK), F32),
                 pltpu.VMEM((ROWS, columns), BF16),
+                pltpu.SMEM((NBLK * EB,), jnp.int32),
+                pltpu.SMEM((NBLK * EB,), F32),
                 pltpu.SemaphoreType.DMA((len(small),)),
                 pltpu.SemaphoreType.DMA((2, 4)),
                 pltpu.SemaphoreType.DMA((NBLK + 2,)),

time: 66.8 us -> 66.8 us (level)
  no operation moved by 1% of the time
where the time goes in v2:
time: 66.8 us; the launch traced here: 66.7 us
  Pallas kernels  63 us (94%)
  local copies, waits for them, and re-layouts  2.3 us (3%)
  between operations  1.3 us (2%)
    pallas_call x1, Pallas kernels, local(): pl.pallas_call(functools.partial(kernel, X, Z, Y), out_shape=jax.ShapeDty...  63 us
    unnamed x1, local copies, waits for them, and re-layouts  2.3 us

profile of v2, /device:TPU:1, one launch (start us, length us, event | category | flops | bytes accessed | tf_op | source)
XLA Modules:
  0.0 66.7 jit_solution(8315696859622432755)
XLA Ops:
  1.3 63.0 %shard_map.154 = bf16[256,2048]{1,0:T(8,128)(2,1)} custom-call(s32[1,16]{1,0:T(1,128)} %refs_0_.1, s32[256]{0:T(256)} %bitcast.14, s32[256]{0:T(256)} %refs_2_.1, s32[1]{0:T(128)S(6)} %copy.18.refs_3_, s32[1]{0:T(128)S(6)} %copy.19.refs_4_, s32[4,32]{1,0:T(4,128)} %bitcast.11, s32[4,32]{1,0:T(4,128)} %bitcast.12, s32[4,32]{1,0:T(4,128)} %bitcast.13, ...), custom_call_target="tpu_custom_call" | custom-call | flops 2200000000 | bytes 3300000 | tf_op jit(solution)/shard_map/pallas_call | solution.py:512
  64.3 2.3 %copy.20 = bf16[2,128,2048]{2,1,0:T(8,128)(2,1)} copy(bf16[2,128,2048]{2,1,0:T(8,128)(2,1)} %bitcast.8) | data formatting | bytes 2097152

commit v3 on v2

--- a/solution.py
+++ b/solution.py
@@ -18,7 +18,7 @@
     4: ((1, 2), (1, 1), (2, 2)),
     8: ((1, 4), (1, 3), (1, 2), (2, 4), (2, 3), (2, 2), (1, 1), (3, 4), (3, 3), (4, 4)),
 }
-IN_FLIGHT = 3
+IN_FLIGHT = 5
 F32 = jnp.float32
 BF16 = jnp.bfloat16
 

time: 66.8 us -> 68.2 us (1.021)
  Pallas kernels: 63 us -> 64.4 us
    pallas_call x1, Pallas kernels: 63 us -> 64.4 us  [local(): pl.pallas_call(functools.partial(kernel, X, Z, Y), out_shape=jax.ShapeDty...]
where the time goes in v3:
time: 68.2 us; the launch traced here: 68.1 us
  Pallas kernels  64.4 us (94%)
  local copies, waits for them, and re-layouts  2.3 us (3%)
  between operations  1.3 us (2%)
    pallas_call x1, Pallas kernels, local(): pl.pallas_call(functools.partial(kernel, X, Z, Y), out_shape=jax.ShapeDty...  64.4 us
    unnamed x1, local copies, waits for them, and re-layouts  2.3 us

profile of v3, /device:TPU:1, one launch (start us, length us, event | category | flops | bytes accessed | tf_op | source)
XLA Modules:
  0.0 68.1 jit_solution(2558048147055929193)
XLA Ops:
  1.3 64.4 %shard_map.154 = bf16[256,2048]{1,0:T(8,128)(2,1)} custom-call(s32[1,16]{1,0:T(1,128)} %refs_0_.1, s32[256]{0:T(256)} %bitcast.14, s32[256]{0:T(256)} %refs_2_.1, s32[1]{0:T(128)S(6)} %copy.18.refs_3_, s32[1]{0:T(128)S(6)} %copy.19.refs_4_, s32[4,32]{1,0:T(4,128)} %bitcast.11, s32[4,32]{1,0:T(4,128)} %bitcast.12, s32[4,32]{1,0:T(4,128)} %bitcast.13, ...), custom_call_target="tpu_custom_call" | custom-call | flops 2200000000 | bytes 3300000 | tf_op jit(solution)/shard_map/pallas_call | solution.py:512
  65.7 2.3 %copy.20 = bf16[2,128,2048]{2,1,0:T(8,128)(2,1)} copy(bf16[2,128,2048]{2,1,0:T(8,128)(2,1)} %bitcast.8) | data formatting | bytes 2097152
